TPU v7x, 512 devices: a whole 4x8x8 slice. The times are simulated.
512 devices in a mesh: dp: 16 (over y, core), seq: 32 (over x, z).
Axes of the slice: x: 4, y: 8, z: 8, core: 2. Of those that a mesh axis runs over, the one named last changes fastest.
Arguments:
- frame_in: bfloat16 [16, 4608, 1024], P('dp', 'seq'), may hold values from -120 to 120
- token_ids: int32 [16, 32, 60], P('dp', 'seq'), may hold values from 0 to 3327
- durations: int32 [16, 32, 60], P('dp', 'seq'), may hold values from 1 to 4, 144 in all within a row
- valid_len: int32 [16], P('dp'), may hold values from 1152 to 4608, as said below
- t_bin: int32 [16], P('dp'), may hold values from 0 to 63
- token_table: bfloat16 [3328, 512], P('seq'), may hold values from -6 to 6
- enc_weight: bfloat16 [512, 1024], replicated, may hold values from -0.25 to 0.25
- mod_table: float32 [64, 2048], replicated, may hold values from -1.2 to 2.5
- w_query: bfloat16 [1024, 512], P('seq'), may hold values from -0.1875 to 0.1875
- w_key: bfloat16 [1024, 512], P('seq'), may hold values from -0.1875 to 0.1875
- w_value: bfloat16 [1024, 512], P('seq'), may hold values from -0.1875 to 0.1875
- attn_grad: bfloat16 [16, 4608, 512], P('dp', 'seq'), may hold values from -6 to 6
Outputs:
- attn_out: bfloat16 [16, 4608, 512], P('dp', 'seq')
- frame_grad: bfloat16 [16, 4608, 1024], P('dp', 'seq')
- query_weight_grad: float32 [1024, 512], P('seq')
- key_weight_grad: float32 [1024, 512], P('seq')
- value_weight_grad: float32 [1024, 512], P('seq')
Inputs may be any that keep to these rules, and one draw needn't show every extreme that they name: In every slab the 60 durations sum to 144, so each token's frames lie in its own slab; some token lasts 4 frames. `valid_len`: some recording is valid over all 4608 frames.
All inputs are finite; a program needn't handle non-finite values.
Results may differ from a plain program's by a relative error of at most 0.017.
The roundings to bfloat16 on the way count: a program that leaves them out, or rounds other values in their place, can miss the bound.
Values may be sent and summed in bfloat16 or wider, within the bound.
A program may use at most 64 MiB of HBM per device.

v0:
```python
import math
import jax
import jax.numpy as jnp
from jax import lax
from jax.sharding import PartitionSpec as P

D = 1024
HEADS = 8
HD = 64
BLK = 48
QW = 512


def extended_2(cells, sides, width):
    for axis, dim in sides:
        count = lax.axis_size(axis)
        ends = count - 1
        head = lax.slice_in_dim(cells, 0, width, axis=dim)
        tail = lax.slice_in_dim(cells, cells.shape[dim] - width, cells.shape[dim], axis=dim)
        cells = jnp.concatenate(
            [
                lax.ppermute(tail, axis, [(i, (i + 1) % count) for i in range(ends)]),
                cells,
                lax.ppermute(head, axis, [((i + 1) % count, i) for i in range(ends)]),
            ],
            axis=dim,
        )
    return cells


def shifted(block, axis, distance):
    devices = range(lax.axis_size(axis))
    route = [(i - distance, i) for i in devices if i - distance in devices]
    return lax.ppermute(block, axis, route)


def attend_window(
    q_blocks, key_ext, value_ext, grad_out, query_pos, key_pos, valid_end, frames_total
):
    n_blocks = q_blocks.shape[0]
    block_len = q_blocks.shape[1]
    key_win = jnp.concatenate([key_ext[offset : offset + n_blocks] for offset in range(4)], axis=1)
    value_win = jnp.concatenate(
        [value_ext[offset : offset + n_blocks] for offset in range(4)], axis=1
    )
    key_here = key_pos[:, None, :]
    allowed = (
        (key_here >= 0)
        & (key_here < frames_total)
        & ((key_here < valid_end) | (query_pos[:, :, None] >= valid_end))
    )
    row_mask = allowed[:, None]
    inv_scale = 1.0 / math.sqrt(q_blocks.shape[-1])
    scores = (
        jnp.einsum("bqhd,bkhd->bhqk", q_blocks, key_win, preferred_element_type=jnp.float32)
        * inv_scale
    )
    scores = jnp.where(row_mask, scores, -1e30)
    row_top = jnp.max(scores, axis=-1, keepdims=True)
    shifted_exp = jnp.where(row_mask, jnp.exp(scores - row_top), 0.0)
    attn_prob = shifted_exp / jnp.sum(shifted_exp, axis=-1, keepdims=True)
    probs_low = attn_prob.astype(jnp.bfloat16)
    mixed_out = jnp.einsum(
        "bhqk,bkhd->bqhd", probs_low, value_win, preferred_element_type=jnp.float32
    ).astype(jnp.bfloat16)
    grad_probs = jnp.einsum(
        "bqhd,bkhd->bhqk", grad_out, value_win, preferred_element_type=jnp.float32
    )
    centre = jnp.sum(attn_prob * grad_probs, axis=-1, keepdims=True)
    grad_scores = (attn_prob * (grad_probs - centre) * inv_scale).astype(jnp.bfloat16)
    grad_query = jnp.einsum(
        "bhqk,bkhd->bqhd", grad_scores, key_win, preferred_element_type=jnp.float32
    ).astype(jnp.bfloat16)
    key_terms = jnp.einsum(
        "bhqk,bqhd->bkhd", grad_scores, q_blocks, preferred_element_type=jnp.float32
    )
    value_terms = jnp.einsum(
        "bhqk,bqhd->bkhd", probs_low, grad_out, preferred_element_type=jnp.float32
    )
    win_terms = jnp.concatenate([key_terms, value_terms], axis=2)
    pieces = win_terms.reshape(n_blocks, 4, block_len, win_terms.shape[2], win_terms.shape[3])
    folded = jnp.zeros((n_blocks + 3,) + pieces.shape[2:], jnp.float32)
    for offset in range(4):
        folded = folded + jnp.pad(pieces[:, offset], ((offset, 3 - offset), (0, 0), (0, 0), (0, 0)))
    return (mixed_out, grad_query, folded)


def pick_rows(wanted, table_piece):
    inside = (wanted >= 0) & (wanted < table_piece.shape[0])
    picked = jnp.take(table_piece, jnp.clip(wanted, 0, table_piece.shape[0] - 1), axis=0)
    return jnp.where(inside[:, None], picked, jnp.zeros_like(picked))


def shards(
    frame_in,
    token_ids,
    durations,
    valid_len,
    t_bin,
    token_table,
    enc_weight,
    mod_table,
    w_query,
    w_key,
    w_value,
    attn_grad,
):
    frames = frame_in[0]
    n_frames = frames.shape[0]
    seq_count = lax.axis_size("seq")
    seq_index = lax.axis_index("seq")
    dp_count = lax.axis_size("dp")
    frames_total = n_frames * seq_count
    valid_end = valid_len[0]
    wanted = token_ids[0, 0]
    token_emb = pick_rows(wanted, lax.all_gather(token_table, "seq", axis=0, tiled=True))
    token_ends = jnp.cumsum(durations[0, 0])
    local_pos = jnp.arange(n_frames, dtype=jnp.int32)
    owner_tok = jnp.sum((token_ends[None, :] <= local_pos[:, None]).astype(jnp.int32), axis=1)
    frame_emb = jnp.take(token_emb, owner_tok, axis=0)
    hidden_in = frames.astype(jnp.float32) + jnp.dot(
        frame_emb, enc_weight, preferred_element_type=jnp.float32
    )
    root_ms = jnp.sqrt(jnp.mean(hidden_in * hidden_in, axis=1, keepdims=True) + 1e-06)
    normed = hidden_in / root_ms
    modulation = lax.dynamic_index_in_dim(mod_table, t_bin[0], 0, keepdims=False)
    gain_part = 1.0 + modulation[:D]
    shift_part = modulation[D:]
    modulated = (normed * gain_part + shift_part).astype(jnp.bfloat16)
    shard_cat = jnp.concatenate([w_query, w_key, w_value], axis=1)
    weights_all = lax.all_gather(shard_cat, "seq", axis=0, tiled=True)
    projected = jnp.dot(modulated, weights_all, preferred_element_type=jnp.float32).astype(
        jnp.bfloat16
    )
    queries = projected[:, :QW]
    keys_values = projected[:, QW:]
    padded = extended_2(keys_values, (("seq", 0),), 2 * BLK)
    extended = padded[: n_frames + 3 * BLK]
    n_blocks = n_frames // BLK
    ext_blocks = extended.reshape(n_blocks + 3, BLK, 2, HEADS, HD)
    global_pos = seq_index * n_frames + local_pos
    query_pos = global_pos.reshape(n_blocks, BLK)
    key_pos = (
        seq_index * n_frames
        + (jnp.arange(n_blocks, dtype=jnp.int32)[:, None] - 2) * BLK
        + jnp.arange(4 * BLK, dtype=jnp.int32)[None, :]
    )
    live_rows = global_pos < valid_end
    grad_live = jnp.where(live_rows[:, None], attn_grad[0], jnp.zeros_like(attn_grad[0]))
    attn_blocks, query_grad, ext_grad = attend_window(
        queries.reshape(n_blocks, BLK, HEADS, HD),
        ext_blocks[:, :, 0],
        ext_blocks[:, :, 1],
        grad_live.reshape(n_blocks, BLK, HEADS, HD),
        query_pos,
        key_pos,
        valid_end,
        frames_total,
    )
    ext_rows = ext_grad.reshape(n_frames + 3 * BLK, 2 * QW)
    from_next = shifted(ext_rows[: 2 * BLK], "seq", -1)
    from_prev = shifted(ext_rows[n_frames + 2 * BLK :], "seq", 1)
    own_rows = ext_rows[2 * BLK : 2 * BLK + n_frames]
    own_rows = (
        own_rows
        + jnp.pad(from_next, ((n_frames - 2 * BLK, 0), (0, 0)))
        + jnp.pad(from_prev, ((0, n_frames - BLK), (0, 0)))
    )
    grad_cat = jnp.concatenate(
        [query_grad.reshape(n_frames, QW), own_rows.astype(jnp.bfloat16)], axis=1
    )
    grad_scale = 1.0 / math.sqrt(dp_count * frames_total)
    per_seq = lax.psum_scatter(
        (
            lax.dot_general(
                modulated, grad_cat, (((0,), (0,)), ((), ())), preferred_element_type=jnp.float32
            )
            * grad_scale
        ).astype(jnp.bfloat16),
        "seq",
        scatter_dimension=0,
        tiled=True,
    ).astype(jnp.float32)
    weight_grad = lax.psum(per_seq, "dp")
    hidden_grad = lax.dot_general(
        grad_cat, weights_all, (((1,), (1,)), ((), ())), preferred_element_type=jnp.float32
    )
    scaled_grad = hidden_grad * gain_part
    frame_grad = (
        scaled_grad - normed * jnp.mean(scaled_grad * normed, axis=1, keepdims=True)
    ) / root_ms
    return (
        attn_blocks.reshape(n_frames, QW)[None],
        frame_grad.astype(jnp.bfloat16)[None],
        weight_grad[:, :QW],
        weight_grad[:, QW : 2 * QW],
        weight_grad[:, 2 * QW :],
    )


def solution(mesh):
    placed = (
        P("dp", "seq", None),
        P("dp", "seq", None),
        P("dp", "seq", None),
        P("dp"),
        P("dp"),
        P("seq", None),
        P(),
        P(),
        P("seq", None),
        P("seq", None),
        P("seq", None),
        P("dp", "seq", None),
    )
    return jax.shard_map(
        shards,
        mesh=mesh,
        in_specs=placed,
        out_specs=(
            P("dp", "seq", None),
            P("dp", "seq", None),
            P("seq", None),
            P("seq", None),
            P("seq", None),
        ),
        check_vma=False,
    )
```

profile of v0, /device:TPU:25, one launch (start us, length us, event | category | flops | bytes accessed | tf_op | source)
XLA Modules:
  0.0 553.6 jit_solution(4595249403937196069)
XLA Ops:
  11.8 1.9 squeeze.30
  16.7 81.7 %all-gather.3.cloned.1.call-done = bf16[3328,512]{1,0:T(8,128)(2,1)} async-done(((bf16[104,512]{1,0:T(8,128)(2,1)}), bf16[3328,512]{1,0:T(8,128)(2,1)}) %all-gather.3.cloned.1.call-update) | async-done | bytes 3407888 | tf_op jit(solution)/shard_map/all_gather | solution.py:116
  98.5 3.1 gather_fusion
  103.1 81.1 %all-gather.5.cloned.1.call-done = bf16[1024,1536]{1,0:T(8,128)(2,1)} async-done(((bf16[32,1536]{1,0:T(8,128)(2,1)}), bf16[1024,1536]{1,0:T(8,128)(2,1)}) %all-gather.5.cloned.1.call-update) | async-done | bytes 3145744 | tf_op jit(solution)/shard_map/all_gather | solution.py:131
  184.2 2.6 convolution_convert_fusion
  186.8 2.8 collective-permute-start
  192.3 3.8 collective-permute-done.1
  199.6 2.1 copy.74
  206.2 3.3 fusion.56
  209.5 2.1 convolution_bitcast_fusion
  211.6 2.0 fusion.24
  213.6 10.4 %convolution_bitcast_fusion.1 = f32[3,192,8,64]{1,3,2,0:T(8,128)} fusion(f32[3,8,48,192]{3,2,1,0:T(8,128)} %fusion.24, bf16[3,48,8,64]{3,2,1,0:T(8,128)(2,1)} %reshape.221, f32[3,8,48,192]{3,2,1,0:T(8,128)} %get-tuple-element.29, f32[3,8,48]{2,1,0:T(8,128)S(1)} %get-tuple-element.28), kind=kOutput, calls=%fused_computation.10 | convolution fusion | flops 29861184 | bytes 3101184 | tf_op jit(solution)/shard_map/bhqk,bqhd->bkhd/dot_general | solution.py:74
  224.0 3.5 pad_maximum_fusion
  227.5 5.9 %copy.64 = f32[3,192,16,64]{3,2,1,0:T(8,128)} copy(f32[3,192,16,64]{1,3,2,0:T(8,128)} %pad_maximum_fusion) | data formatting | bytes 4718592 | tf_op jit(solution)/shard_map/concatenate | solution.py:80
  233.4 2.7 slice_bitcast_fusion.3
  240.0 2.2 slice.152
  244.6 1.8 slice.154
  246.4 4.5 collective-permute-start.3
  250.9 10.3 %fusion.11 = bf16[3,48,8,64]{3,1,2,0:T(8,128)(2,1)S(1)} fusion(f32[3,8,48,192]{3,2,1,0:T(8,128)} %fusion.24, bf16[3,48,8,64]{1,3,2,0:T(8,128)(2,1)} %bitcast.85, bf16[3,48,8,64]{1,3,2,0:T(8,128)(2,1)} %bitcast.80, bf16[3,48,8,64]{1,3,2,0:T(8,128)(2,1)} %bitcast.83, bf16[3,48,8,64]{1,3,2,0:T(8,128)(2,1)} %bitcast.79, ...), kind=kOutput, calls=%fused_computation.28 | convolution fusion | flops 32294208 | bytes 2511360 | tf_op jit(solution)/shard_map/bhqk,bkhd->bqhd/dot_general | solution.py:71
  263.8 2.7 multiply_convert_fusion
  267.9 2.2 fusion.10
  271.0 3.3 multiply_reduce_fusion.1
  275.2 218.2 %reduce-scatter.2.cloned.1.call-done = bf16[32,1536]{1,0:T(8,128)(2,1)} async-done(((bf16[1024,1536]{1,0:T(8,128)(2,1)}), bf16[32,1536]{1,0:T(8,128)(2,1)}) %reduce-scatter.2.cloned.1.call-update) | async-done | bytes 98320 | tf_op jit(solution)/shard_map/reduce_scatter | solution.py:173
  493.4 53.0 %all-reduce.7 = f32[32,1536]{1,0:T(8,128)S(1)} all-reduce(bf16[32,1536]{1,0:T(8,128)(2,1)} %reduce-scatter.2.cloned.1.call-done), channel_id=1, replica_groups=mesh['dp'=16,'seq'=32] {'dp'}, use_global_device_ids=true, to_apply=%region_8.9 | all-reduce | flops 49152 | bytes 294912 | tf_op jit(solution)/shard_map/psum | solution.py:184
  (130 shorter events, 31.1 us)
Async XLA Ops:
  7.2 95.4 %copy-start = (bf16[512,1024]{1,0:T(8,128)(2,1)S(1)}, bf16[512,1024]{1,0:T(8,128)(2,1)}, u32[]{:S(2)}) copy-start(bf16[512,1024]{1,0:T(8,128)(2,1)} %param.18) | copy-start | bytes 3145732
  7.2 91.3 %all-gather.3.cloned.1.call-start = ((), (), s32[]{:S(2)}) async-start(), calls=%async_computation.1 | async-start | bytes 3514368 | tf_op jit(solution)/shard_map/all_gather | solution.py:116
  7.9 176.3 %all-gather.5.cloned.1.call-start = ((), (), s32[]{:S(2)}) async-start(), calls=%async_computation.2 | async-start | bytes 3244032 | tf_op jit(solution)/shard_map/all_gather | solution.py:131
  9.4 484.0 %reduce-scatter.2.cloned.1.call-start = ((), (), s32[]{:S(2)}) async-start(), calls=%async_computation.3 | async-start | bytes 3244032 | tf_op jit(solution)/shard_map/reduce_scatter | solution.py:173
  11.7 90.8 %copy-start.22 = (bf16[1,144,1024]{2,1,0:T(8,128)(2,1)S(1)}, bf16[1,144,1024]{2,1,0:T(8,128)(2,1)}, u32[]{:S(2)}) copy-start(bf16[1,144,1024]{2,1,0:T(8,128)(2,1)} %param.12) | copy-start | bytes 884740
  15.3 168.9 %copy-start.24 = (f32[1,1024]{1,0:T(1,128)}, f32[1,1024]{1,0:T(1,128)S(1)}, u32[]{:S(2)}) copy-start(f32[1,1024]{1,0:T(1,128)S(1)} %get-tuple-element.17) | copy-start | bytes 12292
  15.3 168.9 %copy-start.27 = (f32[1,1024]{1,0:T(1,128)}, f32[1,1024]{1,0:T(1,128)S(1)}, u32[]{:S(2)}) copy-start(f32[1,1024]{1,0:T(1,128)S(1)} %get-tuple-element.18) | copy-start | bytes 12292
  103.1 83.7 %copy-start.6 = (f32[144,1024]{1,0:T(8,128)}, f32[144,1024]{1,0:T(8,128)S(1)}, u32[]{:S(2)}) copy-start(f32[144,1024]{1,0:T(8,128)S(1)} %get-tuple-element.27) | copy-start | bytes 1769476
  103.1 81.1 %copy-start.29 = (f32[144]{0:T(256)}, f32[144]{0:T(256)S(1)}, u32[]{:S(2)}) copy-start(f32[144]{0:T(256)S(1)} %add_sqrt_fusion) | copy-start | bytes 1732
  186.8 5.4 collective-permute-start
  189.7 6.4 %collective-permute-start.1 = (bf16[96,1024]{1,0:T(8,128)(2,1)S(1)}, bf16[96,1024]{1,0:T(8,128)(2,1)S(1)}, u32[]{:S(2)}, u32[]{:S(2)}) collective-permute-start(bf16[96,1024]{1,0:T(8,128)(2,1)S(1)} %get-tuple-element.20), channel_id=1, source_target_pairs={{1,0},{2,1},{3,2},{4,3},{5,4},{6,5},{7,6},{8,7},{9,8},{10,9},{11,1... | collective-permute-start | bytes 589832 | tf_op jit(solution)/shard_map/ppermute | solution.py:24
  198.3 3.3 copy-start.9
  198.3 4.3 copy-start.8
  199.6 6.6 %copy-start.18 = (bf16[3,48,1,8,64]{1,4,3,0,2:T(8,128)(2,1)}, bf16[3,48,1,8,64]{1,4,3,0,2:T(8,128)(2,1)S(1)}, u32[]{:S(2)}) copy-start(bf16[3,48,1,8,64]{1,4,3,0,2:T(8,128)(2,1)S(1)} %copy.72) | copy-start | bytes 442372
  204.9 6.7 %copy-start.14 = (bf16[3,48,1,8,64]{1,4,3,0,2:T(8,128)(2,1)}, bf16[3,48,1,8,64]{1,4,3,0,2:T(8,128)(2,1)S(1)}, u32[]{:S(2)}) copy-start(bf16[3,48,1,8,64]{1,4,3,0,2:T(8,128)(2,1)S(1)} %copy.69) | copy-start | bytes 442372
  206.2 3.3 copy-start.20
  209.5 4.1 copy-start.32
  242.1 19.7 %collective-permute-start.2 = (f32[96,1024]{1,0:T(8,128)}, f32[96,1024]{1,0:T(8,128)}, u32[]{:S(2)}, u32[]{:S(2)}) collective-permute-start(f32[96,1024]{1,0:T(8,128)} %slice.152), channel_id=1, source_target_pairs={{1,0},{2,1},{3,2},{4,3},{5,4},{6,5},{7,6},{8,7},{9,8},{10,9},{11,1... | collective-permute-start | bytes 1179656 | tf_op jit(solution)/shard_map/ppermute | solution.py:34
  243.8 7.1 %copy-start.33 = (f32[3,8,48]{2,1,0:T(8,128)S(1)}, f32[3,8,48]{2,1,0:T(8,128)}, u32[]{:S(2)}) copy-start(f32[3,8,48]{2,1,0:T(8,128)} %copy-done.32) | copy-start | bytes 13828
  246.4 15.5 %collective-permute-start.3 = (f32[48,1024]{1,0:T(8,128)}, f32[48,1024]{1,0:T(8,128)}, u32[]{:S(2)}, u32[]{:S(2)}) collective-permute-start(f32[48,1024]{1,0:T(8,128)} %slice.154), channel_id=1, source_target_pairs={{0,1},{1,2},{2,3},{3,4},{4,5},{5,6},{6,7},{7,8},{8,9},{9,10},{10,1... | collective-permute-start | bytes 589832 | tf_op jit(solution)/shard_map/ppermute | solution.py:34
  250.9 10.6 %slice-start = ((f32[6,48,16,64]{3,2,1,0:T(8,128)}), f32[3,48,16,64]{3,2,1,0:T(8,128)S(1)}, s32[]{:S(2)}) async-start(f32[6,48,16,64]{3,2,1,0:T(8,128)} %copy-done.5), calls=%async_computation.4 | async-start | bytes 2359296 | tf_op jit(solution)/shard_map/slice | solution.py:163
  261.4 2.3 copy-start.7
  267.9 3.2 copy-start.26
  267.9 3.2 copy-start.31
  (19 other events, 29.5 us)
Sparse Core Ops, SparseCore 0:
  11.2 87.2 all-gather.2
  102.2 81.9 all-gather.4
  266.7 226.6 reduce-scatter.1
where the time goes:
time: 555 us; the launch traced here: 554 us
  waiting for transfers between devices  386 us (70%)
  blocking collectives  53 us (10%)
  matrix products  39.3 us (7%)
  local copies, waits for them, and re-layouts  38.3 us (7%)
  between operations  15.5 us (3%)
  other arithmetic  11.6 us (2%)
  starting transfers between devices  10.3 us (2%)
    reduce_scatter x1, waiting for transfers between devices, shards(): lax.psum_scatter((lax.dot_general(modulated, grad_cat, (((0,), (0,)), (()...  218 us
    all_gather x1, waiting for transfers between devices, shards(): lax.all_gather(token_table, 'seq', axis=0, tiled=True)  81.7 us
    all_gather x1, waiting for transfers between devices, shards(): weights_all = lax.all_gather(shard_cat, 'seq', axis=0, tiled=True)  81.1 us
    psum x1, blocking collectives, shards(): weight_grad = lax.psum(per_seq, 'dp')  53 us
    unnamed x78, local copies, waits for them, and re-layouts  12.7 us
  transfers between devices with their start and end apart: 7, of which 4 were waited for; matrix products, arithmetic and copies ran while one was open for 6% of the time, Pallas kernels for 0%

commit v1 on v0

--- a/solution.py
+++ b/solution.py
@@ -128,7 +128,16 @@
     shift_part = modulation[D:]
     modulated = (normed * gain_part + shift_part).astype(jnp.bfloat16)
     shard_cat = jnp.concatenate([w_query, w_key, w_value], axis=1)
-    weights_all = lax.all_gather(shard_cat, "seq", axis=0, tiled=True)
+    _get_rounds = lambda my_tile: jnp.concatenate(
+        lax.all_to_all(
+            jnp.stack([my_tile for _ in range(lax.axis_size("seq"))], axis=0),
+            axis_name="seq",
+            split_axis=0,
+            concat_axis=0,
+        ),
+        0,
+    )
+    weights_all = _get_rounds(shard_cat)
     projected = jnp.dot(modulated, weights_all, preferred_element_type=jnp.float32).astype(
         jnp.bfloat16
     )

time: 555 us -> 495 us (0.89)
  waiting for transfers between devices: 386 us -> 314 us
  starting transfers between devices: 10.3 us -> 23.1 us
    all_gather x1 -> x0, waiting for transfers between devices: 81.1 us -> none  [shards(): weights_all = lax.all_gather(shard_cat, 'seq', axis=0, tiled=True)]
    all_to_all x0 -> x1, starting transfers between devices: none -> 13.1 us  [shards(): lax.all_to_all(jnp.stack([my_tile for _ in range(lax.axis_size('seq'))],...]
    all_gather x1, waiting for transfers between devices: 81.7 us -> 91.2 us  [shards(): lax.all_gather(token_table, 'seq', axis=0, tiled=True)]
    unnamed x78 -> x84, local copies, waits for them, and re-layouts: 12.7 us -> 13.3 us
  transfers between devices with their start and end apart: 7 -> 7, of which waited for: 4 -> 3; matrix products, arithmetic and copies ran while one was open for 6% -> 6% of each run, Pallas kernels for 0% -> 0%
where the time goes in v1:
time: 495 us; the launch traced here: 494 us
  waiting for transfers between devices  314 us (63%)
  blocking collectives  53.1 us (11%)
  local copies, waits for them, and re-layouts  39.4 us (8%)
  matrix products  39.3 us (8%)
  starting transfers between devices  23.1 us (5%)
  between operations  15.9 us (3%)
  other arithmetic  8.97 us (2%)
    reduce_scatter x1, waiting for transfers between devices, shards(): lax.psum_scatter((lax.dot_general(modulated, grad_cat, (((0,), (0,)), (()...  218 us
    all_gather x1, waiting for transfers between devices, shards(): lax.all_gather(token_table, 'seq', axis=0, tiled=True)  91.2 us
    psum x1, blocking collectives, shards(): weight_grad = lax.psum(per_seq, 'dp')  53.1 us
    unnamed x84, local copies, waits for them, and re-layouts  13.3 us
    all_to_all x1, starting transfers between devices, shards(): lax.all_to_all(jnp.stack([my_tile for _ in range(lax.axis_size('seq'))],...  13.1 us
    dot_general x1, matrix products, attend_window(): jnp.einsum('bhqk,bqhd->bkhd', grad_scores, q_blocks, preferred_element_ty...  10.5 us
    dot_general x1, matrix products, attend_window(): jnp.einsum('bhqk,bkhd->bqhd', grad_scores, key_win, preferred_element_typ...  10.3 us
  transfers between devices with their start and end apart: 7, of which 3 were waited for; matrix products, arithmetic and copies ran while one was open for 6% of the time, Pallas kernels for 0%

profile of v1, /device:TPU:25, one launch (start us, length us, event | category | flops | bytes accessed | tf_op | source)
XLA Modules:
  0.0 493.8 jit_solution(15608763390817869144)
XLA Ops:
  8.7 2.1 stack.2
  10.8 13.1 %all-to-all-start = ((bf16[32,32,1536]{2,1,0:T(8,128)(2,1)}), bf16[32,32,1536]{2,1,0:T(8,128)(2,1)}, u32[]{:S(2)}, u32[]{:S(2)}) async-start(bf16[32,32,1536]{2,1,0:T(8,128)(2,1)} %stack.2), calls=%async_computation | async-start | bytes 6291456 | tf_op jit(solution)/shard_map/all_to_all | solution.py:132
  27.8 91.2 %all-gather.2.cloned.1.call-done = bf16[3328,512]{1,0:T(8,128)(2,1)} async-done(((bf16[104,512]{1,0:T(8,128)(2,1)}), bf16[3328,512]{1,0:T(8,128)(2,1)}) %all-gather.2.cloned.1.call-update) | async-done | bytes 3407888 | tf_op jit(solution)/shard_map/all_gather | solution.py:116
  118.9 3.1 gather_fusion
  124.2 2.6 convolution_convert_fusion
  126.8 2.2 collective-permute-start
  131.6 4.2 collective-permute-done.1
  139.3 2.1 copy.74
  145.9 3.3 fusion.56
  149.2 2.1 convolution_bitcast_fusion
  151.3 2.0 fusion.24
  153.3 10.5 %convolution_bitcast_fusion.1 = f32[3,192,8,64]{1,3,2,0:T(8,128)} fusion(f32[3,8,48,192]{3,2,1,0:T(8,128)} %fusion.24, bf16[3,48,8,64]{3,2,1,0:T(8,128)(2,1)} %reshape.227, f32[3,8,48,192]{3,2,1,0:T(8,128)} %get-tuple-element.29, f32[3,8,48]{2,1,0:T(8,128)S(1)} %get-tuple-element.28), kind=kOutput, calls=%fused_computation.10 | convolution fusion | flops 29861184 | bytes 3101184 | tf_op jit(solution)/shard_map/bhqk,bqhd->bkhd/dot_general | solution.py:74
  163.7 3.5 pad_maximum_fusion
  167.2 5.9 %copy.64 = f32[3,192,16,64]{3,2,1,0:T(8,128)} copy(f32[3,192,16,64]{1,3,2,0:T(8,128)} %pad_maximum_fusion) | data formatting | bytes 4718592 | tf_op jit(solution)/shard_map/concatenate | solution.py:80
  173.1 2.7 slice_bitcast_fusion.3
  179.7 2.1 slice.152
  184.3 1.8 slice.154
  186.1 4.8 collective-permute-start.3
  190.8 10.3 %fusion.11 = bf16[3,48,8,64]{3,1,2,0:T(8,128)(2,1)S(1)} fusion(f32[3,8,48,192]{3,2,1,0:T(8,128)} %fusion.24, bf16[3,48,8,64]{1,3,2,0:T(8,128)(2,1)} %bitcast.86, bf16[3,48,8,64]{1,3,2,0:T(8,128)(2,1)} %bitcast.81, bf16[3,48,8,64]{1,3,2,0:T(8,128)(2,1)} %bitcast.84, bf16[3,48,8,64]{1,3,2,0:T(8,128)(2,1)} %bitcast.80, ...), kind=kOutput, calls=%fused_computation.28 | convolution fusion | flops 32294208 | bytes 2511360 | tf_op jit(solution)/shard_map/bhqk,bkhd->bqhd/dot_general | solution.py:71
  203.7 2.7 multiply_convert_fusion
  207.8 2.2 fusion.10
  211.0 3.3 multiply_reduce_fusion.1
  215.2 218.0 %reduce-scatter.2.cloned.1.call-done = bf16[32,1536]{1,0:T(8,128)(2,1)} async-done(((bf16[1024,1536]{1,0:T(8,128)(2,1)}), bf16[32,1536]{1,0:T(8,128)(2,1)}) %reduce-scatter.2.cloned.1.call-update) | async-done | bytes 98320 | tf_op jit(solution)/shard_map/reduce_scatter | solution.py:182
  433.2 53.1 %all-reduce.7 = f32[32,1536]{1,0:T(8,128)S(1)} all-reduce(bf16[32,1536]{1,0:T(8,128)(2,1)} %reduce-scatter.2.cloned.1.call-done), channel_id=1, replica_groups=mesh['dp'=16,'seq'=32] {'dp'}, use_global_device_ids=true, to_apply=%region_8.9 | all-reduce | flops 49152 | bytes 294912 | tf_op jit(solution)/shard_map/psum | solution.py:193
  (136 shorter events, 29.2 us)
Async XLA Ops:
  7.2 115.9 %copy-start = (bf16[512,1024]{1,0:T(8,128)(2,1)S(1)}, bf16[512,1024]{1,0:T(8,128)(2,1)}, u32[]{:S(2)}) copy-start(bf16[512,1024]{1,0:T(8,128)(2,1)} %param.18) | copy-start | bytes 3145732
  7.2 111.7 %all-gather.2.cloned.1.call-start = ((), (), s32[]{:S(2)}) async-start(), calls=%async_computation.2 | async-start | bytes 3514368 | tf_op jit(solution)/shard_map/all_gather | solution.py:116
  10.8 14.5 %copy-start.33 = (s32[1,1,60]{2,1,0:T(1,128)S(1)}, s32[1,1,60]{2,1,0:T(1,128)}, u32[]{:S(2)}) copy-start(s32[1,1,60]{2,1,0:T(1,128)} %param.14) | copy-start | bytes 724
  10.8 14.8 %copy-start.24 = (bf16[1,144,512]{2,1,0:T(8,128)(2,1)S(1)}, bf16[1,144,512]{2,1,0:T(8,128)(2,1)}, u32[]{:S(2)}) copy-start(bf16[1,144,512]{2,1,0:T(8,128)(2,1)} %param.23) | copy-start | bytes 442372
  10.8 15.8 %copy-start.34 = (s32[1,1,60]{2,1,0:T(1,128)S(1)}, s32[1,1,60]{2,1,0:T(1,128)}, u32[]{:S(2)}) copy-start(s32[1,1,60]{2,1,0:T(1,128)} %param.13) | copy-start | bytes 724
  10.8 112.7 %all-to-all-start = ((bf16[32,32,1536]{2,1,0:T(8,128)(2,1)}), bf16[32,32,1536]{2,1,0:T(8,128)(2,1)}, u32[]{:S(2)}, u32[]{:S(2)}) async-start(bf16[32,32,1536]{2,1,0:T(8,128)(2,1)} %stack.2), calls=%async_computation | async-start | bytes 6291456 | tf_op jit(solution)/shard_map/all_to_all | solution.py:132
  24.0 409.2 %reduce-scatter.2.cloned.1.call-start = ((), (), s32[]{:S(2)}) async-start(), calls=%async_computation.3 | async-start | bytes 3244032 | tf_op jit(solution)/shard_map/reduce_scatter | solution.py:182
  25.7 97.4 %copy-start.22 = (bf16[1,144,1024]{2,1,0:T(8,128)(2,1)S(1)}, bf16[1,144,1024]{2,1,0:T(8,128)(2,1)}, u32[]{:S(2)}) copy-start(bf16[1,144,1024]{2,1,0:T(8,128)(2,1)} %param.12) | copy-start | bytes 884740
  27.6 96.0 %copy-start.25 = (f32[1,1024]{1,0:T(1,128)}, f32[1,1024]{1,0:T(1,128)S(1)}, u32[]{:S(2)}) copy-start(f32[1,1024]{1,0:T(1,128)S(1)} %get-tuple-element.17) | copy-start | bytes 12292
  27.6 96.0 %copy-start.28 = (f32[1,1024]{1,0:T(1,128)}, f32[1,1024]{1,0:T(1,128)S(1)}, u32[]{:S(2)}) copy-start(f32[1,1024]{1,0:T(1,128)S(1)} %get-tuple-element.18) | copy-start | bytes 12292
  123.5 3.2 copy-start.6
  126.8 4.8 collective-permute-start
  129.0 6.8 %collective-permute-start.1 = (bf16[96,1024]{1,0:T(8,128)(2,1)S(1)}, bf16[96,1024]{1,0:T(8,128)(2,1)S(1)}, u32[]{:S(2)}, u32[]{:S(2)}) collective-permute-start(bf16[96,1024]{1,0:T(8,128)(2,1)S(1)} %get-tuple-element.20), channel_id=1, source_target_pairs={{1,0},{2,1},{3,2},{4,3},{5,4},{6,5},{7,6},{8,7},{9,8},{10,9},{11,1... | collective-permute-start | bytes 589832 | tf_op jit(solution)/shard_map/ppermute | solution.py:24
  138.0 3.4 copy-start.9
  138.0 4.3 copy-start.8
  139.3 6.6 %copy-start.18 = (bf16[3,48,1,8,64]{1,4,3,0,2:T(8,128)(2,1)}, bf16[3,48,1,8,64]{1,4,3,0,2:T(8,128)(2,1)S(1)}, u32[]{:S(2)}) copy-start(bf16[3,48,1,8,64]{1,4,3,0,2:T(8,128)(2,1)S(1)} %copy.72) | copy-start | bytes 442372
  144.6 6.7 %copy-start.14 = (bf16[3,48,1,8,64]{1,4,3,0,2:T(8,128)(2,1)}, bf16[3,48,1,8,64]{1,4,3,0,2:T(8,128)(2,1)S(1)}, u32[]{:S(2)}) copy-start(bf16[3,48,1,8,64]{1,4,3,0,2:T(8,128)(2,1)S(1)} %copy.69) | copy-start | bytes 442372
  145.9 3.3 copy-start.20
  149.2 4.1 copy-start.35
  181.8 20.0 %collective-permute-start.2 = (f32[96,1024]{1,0:T(8,128)}, f32[96,1024]{1,0:T(8,128)}, u32[]{:S(2)}, u32[]{:S(2)}) collective-permute-start(f32[96,1024]{1,0:T(8,128)} %slice.152), channel_id=1, source_target_pairs={{1,0},{2,1},{3,2},{4,3},{5,4},{6,5},{7,6},{8,7},{9,8},{10,9},{11,1... | collective-permute-start | bytes 1179656 | tf_op jit(solution)/shard_map/ppermute | solution.py:34
  183.4 7.4 %copy-start.36 = (f32[3,8,48]{2,1,0:T(8,128)S(1)}, f32[3,8,48]{2,1,0:T(8,128)}, u32[]{:S(2)}) copy-start(f32[3,8,48]{2,1,0:T(8,128)} %copy-done.35) | copy-start | bytes 13828
  186.1 15.8 %collective-permute-start.3 = (f32[48,1024]{1,0:T(8,128)}, f32[48,1024]{1,0:T(8,128)}, u32[]{:S(2)}, u32[]{:S(2)}) collective-permute-start(f32[48,1024]{1,0:T(8,128)} %slice.154), channel_id=1, source_target_pairs={{0,1},{1,2},{2,3},{3,4},{4,5},{5,6},{6,7},{7,8},{8,9},{9,10},{10,1... | collective-permute-start | bytes 589832 | tf_op jit(solution)/shard_map/ppermute | solution.py:34
  190.8 10.6 %slice-start = ((f32[6,48,16,64]{3,2,1,0:T(8,128)}), f32[3,48,16,64]{3,2,1,0:T(8,128)S(1)}, s32[]{:S(2)}) async-start(f32[6,48,16,64]{3,2,1,0:T(8,128)} %copy-done.5), calls=%async_computation.4 | async-start | bytes 2359296 | tf_op jit(solution)/shard_map/slice | solution.py:172
  207.8 3.2 copy-start.32
  (22 other events, 35.6 us)
Sparse Core Ops, SparseCore 0:
  11.2 107.7 all-gather.1
  206.7 226.4 reduce-scatter.1
